TPU v7x, 256 devices: a whole 4x4x8 slice. The times are simulated.
256 devices in a mesh: band: 4 (over x), py: 4 (over z_hi), pz: 16 (over z_lo, y, core).
Axes of the slice: x: 4, y: 4, z: 8 (z_hi: 4, z_lo: 2; z = z_hi * 2 + z_lo), core: 2. Of those that a mesh axis runs over, the one named last changes fastest.
Arguments:
- coefficients: float32 [8, 256, 256, 256], P('band', 'pz', 'py'), parts along dimension 0, may hold values from -6 to 6
- potential: float32 [256, 256, 256], P('pz', 'py'), may hold values from -6 to 6
- column_limit: int32 [256, 256], P('pz', 'py'), may hold values from -1 to 96, as said below
- entry_atom: int32 [32768, 1], P(('py', 'pz')), may hold values from 0 to 4095, as said below
- entry_block: int32 [32768], P(('py', 'pz')), may hold values from 0 to 2047, as said below
- projectors: float32 [32768, 8, 128], P(('py', 'pz')), may hold values from -0.6 to 0.6
- coupling: float32 [8, 8], replicated, may hold values from -4 to 4
Outputs:
- applied: float32 [8, 256, 256, 256], P('band', 'pz', 'py'), parts along dimension 0
There are 4 independent parts, one for each index of `band`. A program takes and returns all parts, laid end to end along the dimension named above; an argument that names none is the same for every part. Nothing has to cross between parts.
Inputs may be any that keep to these rules, and one draw needn't show every extreme that they name: column_limit[y, x] = (number of k in 0..128 with k^2 + freq(y)^2 + freq(x)^2 + j <= 96^2) - 1, with j in 0..2 drawn for each column and 0 at column (0, 0); -1 marks an empty column. `entry_atom`: atom a is centred on device a // (4096 / (4 * 16)); an entry of device (p, q) names an atom centred on (p, q) or on one of its four neighbours (p - 1, q), (p + 1, q), (p, q - 1), (p, q + 1), indices taken modulo 4 and 16; the first 4096 / (4 * 16) entries of each device name its own atoms in order. `entry_block`: the blocks of one atom's entries lie within four blocks of one centre block of that atom, modulo 2048.
All inputs are finite; a program needn't handle non-finite values.
Results may differ from a plain program's by a relative error of at most 0.00007.
Values sent between devices are 32-bit elements; how exact they have to be, the bound alone decides.
A program may use at most 128 MiB of HBM per device.

v0:
```python
import functools
import math

import jax
import jax.numpy as jnp
from jax import lax
from jax.sharding import PartitionSpec as P

BLOCK = 128
NATOM = 4096


HIGHEST_MODE = lax.Precision.HIGHEST


def cas_table(points):
    indices = jnp.arange(points, dtype=jnp.int32)
    product = indices[:, None] * indices[None, :] % points
    angles = product.astype(jnp.float32) * (2.0 * math.pi / points)
    return (jnp.cos(angles) + jnp.sin(angles)) / math.sqrt(points)


def frequency(indices, points):
    return jnp.minimum(indices, points - indices)


def along_depth(hartley, values):
    return jnp.einsum("ka,nayx->nkyx", hartley, values, precision=HIGHEST_MODE)


def along_rows(hartley, values):
    return jnp.einsum("ka,nzax->nzkx", hartley, values, precision=HIGHEST_MODE)


def along_width(hartley, values):
    return jnp.einsum("ka,nzya->nzyk", hartley, values, precision=HIGHEST_MODE)


def real_space(spectrum, hartley, first_move, second_move):
    depth_done = along_depth(hartley, spectrum)
    rows_done = first_move(depth_done, functools.partial(along_rows, hartley))
    return second_move(rows_done, functools.partial(along_width, hartley))


def spectral(values, hartley, first_move, second_move):
    width_done = along_width(hartley, values)
    rows_done = first_move(width_done, functools.partial(along_rows, hartley))
    return second_move(rows_done, functools.partial(along_depth, hartley))


def shards(coefficients, potential, column_limit, entry_atom, entry_block, projectors, coupling):
    band_count, rows_local, width_local, grid_points = coefficients.shape
    hartley = cas_table(grid_points)
    row_group = lax.axis_index("pz")
    width_group = lax.axis_index("py")
    depth_freq = frequency(jnp.arange(grid_points, dtype=jnp.int32), grid_points)
    rows_freq = frequency(
        row_group * rows_local + jnp.arange(rows_local, dtype=jnp.int32), grid_points
    )
    width_freq = frequency(
        width_group * width_local + jnp.arange(width_local, dtype=jnp.int32), grid_points
    )
    sphere = (depth_freq[None, None, :] <= column_limit[:, :, None]).astype(jnp.float32)
    squared = (
        rows_freq[:, None, None] ** 2
        + width_freq[None, :, None] ** 2
        + depth_freq[None, None, :] ** 2
    )
    kinetic = 0.5 * squared.astype(jnp.float32) * (4.0 / grid_points) ** 2
    masked = coefficients * sphere[None]
    start = jnp.transpose(masked, (0, 3, 1, 2))
    real_field = jnp.concatenate(
        [
            real_space(
                start[single : single + 1],
                hartley,
                lambda values, handler: handler(
                    lax.all_to_all(values, "pz", split_axis=1, concat_axis=2, tiled=True)
                ),
                lambda values, handler: handler(
                    lax.all_to_all(values, "py", split_axis=2, concat_axis=3, tiled=True)
                ),
            )
            for single in range(band_count)
        ],
        axis=0,
    )
    block_count = real_field.shape[1] * real_field.shape[2] * real_field.shape[3] // BLOCK
    blocks = real_field.reshape(band_count, block_count, BLOCK)
    gathered = blocks[:, entry_block, :]
    partial_terms = jnp.einsum("epc,nec->epn", projectors, gathered, precision=HIGHEST_MODE)
    symmetric = 0.5 * (coupling + coupling.T)
    atoms = entry_atom[:, 0]
    atom_terms = jax.ops.segment_sum(partial_terms, atoms, num_segments=NATOM)
    totals = lax.psum(atom_terms, ("py", "pz"))
    coupled = jnp.einsum("qp,apn->aqn", symmetric, totals, precision=HIGHEST_MODE)
    selected = coupled[atoms]
    spread = jnp.einsum("epc,epn->enc", projectors, selected, precision=HIGHEST_MODE)
    placed = jax.ops.segment_sum(spread, entry_block, num_segments=block_count)
    projected = jnp.moveaxis(placed, 1, 0).reshape(real_field.shape)
    total = potential[None] * real_field + projected
    back = jnp.concatenate(
        [
            spectral(
                total[single : single + 1],
                hartley,
                lambda values, handler: handler(
                    lax.all_to_all(values, "py", split_axis=3, concat_axis=2, tiled=True)
                ),
                lambda values, handler: handler(
                    lax.all_to_all(values, "pz", split_axis=2, concat_axis=1, tiled=True)
                ),
            )
            for single in range(band_count)
        ],
        axis=0,
    )
    back = jnp.transpose(back, (0, 2, 3, 1))
    return sphere[None] * (kinetic[None] * masked + back)


def solution(mesh):
    in_specs = (
        P("band", "pz", "py", None),
        P("pz", "py", None),
        P("pz", "py"),
        P(("py", "pz"), None),
        P(("py", "pz")),
        P(("py", "pz"), None, None),
        P(),
    )
    out_specs = P("band", "pz", "py", None)
    return jax.shard_map(shards, mesh=mesh, in_specs=in_specs, out_specs=out_specs, check_vma=False)
```

profile of v0, /device:TPU:1, one launch (start us, length us, event | category | flops | bytes accessed | tf_op | source)
XLA Modules:
  0.0 571.2 jit_solution(10152489785589529890)
XLA Ops:
  7.6 2.3 multiply_bitcast_fusion
  13.3 2.5 copy.65
  15.8 3.4 reshape.182
  19.2 7.3 %all-to-all-start = ((f32[16,1,16384]{2,1,0:T(1,128)}), f32[16,1,16384]{2,1,0:T(1,128)}, u32[]{:S(2)}, u32[]{:S(2)}) async-start(f32[16,1,16384]{2,1,0:T(1,128)} %reshape.182), calls=%async_computation | async-start | bytes 2097152 | tf_op jit(solution)/shard_map/all_to_all | solution.py:78
  26.5 3.3 convolution_bitcast_fusion.7
  29.8 2.5 copy.70
  32.3 3.4 reshape.178
  35.7 6.8 %all-to-all-done = f32[16,1,16384]{2,1,0:T(1,128)} async-done(((f32[16,1,16384]{2,1,0:T(1,128)}), f32[16,1,16384]{2,1,0:T(1,128)}, u32[]{:S(2)}, u32[]{:S(2)}) %all-to-all-start) | async-done | bytes 1048608 | tf_op jit(solution)/shard_map/all_to_all | solution.py:78
  42.5 5.5 all-to-all-start.2
  48.6 4.4 reduce.2
  53.0 2.2 reshape.183
  57.0 4.3 convolution_bitcast_fusion.2
  61.3 2.5 copy.68
  63.8 4.2 reshape.184
  68.0 7.4 %all-to-all-start.1 = ((f32[4,1,65536]{2,1,0:T(1,128)}), f32[4,1,65536]{2,1,0:T(1,128)}, u32[]{:S(2)}, u32[]{:S(2)}) async-start(f32[4,1,65536]{2,1,0:T(1,128)} %reshape.184), calls=%async_computation.1 | async-start | bytes 2097152 | tf_op jit(solution)/shard_map/all_to_all | solution.py:81
  75.4 4.4 reduce
  83.7 4.3 convolution_bitcast_fusion.1
  88.1 2.5 copy.73
  90.6 4.2 reshape.180
  94.8 10.8 %all-to-all-start.3 = ((f32[4,1,65536]{2,1,0:T(1,128)}), f32[4,1,65536]{2,1,0:T(1,128)}, u32[]{:S(2)}, u32[]{:S(2)}) async-start(f32[4,1,65536]{2,1,0:T(1,128)} %reshape.180), calls=%async_computation.3 | async-start | bytes 2097152 | tf_op jit(solution)/shard_map/all_to_all | solution.py:81
  105.6 4.6 reduce.3
  110.2 2.3 reshape.185
  112.5 4.3 copy.110
  116.8 3.4 reshape.131
  120.2 3.3 fusion.27
  124.6 5.6 reduce.1
  130.1 3.5 reshape.181
  133.7 4.3 copy.109
  137.9 3.6 reshape.134
  141.5 3.3 fusion.23
  145.9 4.1 pad_maximum_fusion
  150.0 3.8 gather_fusion
  153.8 4.4 convolution_bitcast_fusion.9
  158.3 2.9 broadcast_in_dim.10
  161.2 49.1 %scatter_fusion = f32[4096,8,2]{1,2,0:T(2,128)} fusion(f32[4096,8,2]{1,2,0:T(2,128)} %broadcast_in_dim.10, s32[512]{0:T(512)S(1)} %bitcast.198, f32[512,8,2]{1,2,0:T(2,128)S(1)} %convolution_bitcast_fusion.9), kind=kCustom, calls=%fused_computation.2 | custom fusion | flops 8192 | bytes 100352 | tf_op jit(solution)/shard_map/scatter-add | solution.py:94
  210.3 5.8 %copy.77 = f32[4096,8,2]{0,1,2:T(8,128)} copy(f32[4096,8,2]{1,2,0:T(2,128)} %scatter_fusion) | data formatting | bytes 524288 | tf_op jit(solution)/shard_map/scatter-add | solution.py:94
  216.2 183.2 %all-reduce.2.cloned.1.call-done = f32[4096,8,2]{0,1,2:T(8,128)} async-done(((f32[4096,8,2]{0,1,2:T(8,128)}), f32[4096,8,2]{0,1,2:T(8,128)}) %all-reduce.2.cloned.1.call-update) | async-done | bytes 262160 | tf_op jit(solution)/shard_map/psum | solution.py:95
  400.7 4.5 copy.79
  405.2 3.7 gather_fusion.1
  408.9 3.4 fusion.102
  412.9 16.7 %scatter_fusion.1 = f32[2048,2,128]{2,1,0:T(2,128)S(1)} fusion(f32[2048,2,128]{2,1,0:T(2,128)S(1)} %broadcast_in_dim.8, s32[512]{0:T(512)S(1)} %copy-done.17, f32[512,2,128]{2,1,0:T(2,128)S(1)} %fusion.102), kind=kCustom, calls=%fused_computation.3 | custom fusion | flops 131072 | bytes 1574912 | tf_op jit(solution)/shard_map/scatter-add | solution.py:99
  431.0 3.0 reshape.135
  439.5 2.5 copy.81
  441.9 4.3 reshape.190
  446.3 4.2 all-to-all-start.4
  453.9 2.4 reshape.186
  456.3 19.8 %all-to-all-done.4 = f32[4,1,65536]{2,1,0:T(1,128)} async-done(((f32[4,1,65536]{2,1,0:T(1,128)}), f32[4,1,65536]{2,1,0:T(1,128)}, u32[]{:S(2)}, u32[]{:S(2)}) %all-to-all-start.4) | async-done | bytes 1048608 | tf_op jit(solution)/shard_map/all_to_all | solution.py:108
  476.2 4.9 all-to-all-start.6
  481.1 4.6 reduce.6
  486.7 2.7 copy.108
  489.4 2.5 reshape.137
  495.3 2.3 reshape.192
  497.5 9.9 %all-to-all-done.6 = f32[4,1,65536]{2,1,0:T(1,128)} async-done(((f32[4,1,65536]{2,1,0:T(1,128)}), f32[4,1,65536]{2,1,0:T(1,128)}, u32[]{:S(2)}, u32[]{:S(2)}) %all-to-all-start.6) | async-done | bytes 1048608 | tf_op jit(solution)/shard_map/all_to_all | solution.py:108
  507.5 5.3 all-to-all-start.5
  512.8 4.6 reduce.4
  518.4 2.7 copy.107
  521.1 2.5 reshape.140
  526.9 2.3 reshape.188
  529.2 5.9 %all-to-all-start.7 = ((f32[16,1,16384]{2,1,0:T(1,128)}), f32[16,1,16384]{2,1,0:T(1,128)}, u32[]{:S(2)}, u32[]{:S(2)}) async-start(f32[16,1,16384]{2,1,0:T(1,128)} %reshape.188), calls=%async_computation.7 | async-start | bytes 2097152 | tf_op jit(solution)/shard_map/all_to_all | solution.py:111
  536.4 4.4 reduce.7
  542.6 5.7 fusion.7
  548.2 2.7 all-to-all-done.7
  550.9 4.4 reduce.5
  557.3 4.6 fusion.10
  (81 shorter events, 40.8 us)
Async XLA Ops:
  6.5 147.3 %copy-start = (f32[512,8,128]{2,1,0:T(8,128)S(1)}, f32[512,8,128]{2,1,0:T(8,128)}, u32[]{:S(2)}) copy-start(f32[512,8,128]{2,1,0:T(8,128)} %param.12) | copy-start | bytes 6291460
  7.6 2.3 copy-start.6
  9.9 1.3 copy-start.10
  19.2 23.3 %all-to-all-start = ((f32[16,1,16384]{2,1,0:T(1,128)}), f32[16,1,16384]{2,1,0:T(1,128)}, u32[]{:S(2)}, u32[]{:S(2)}) async-start(f32[16,1,16384]{2,1,0:T(1,128)} %reshape.182), calls=%async_computation | async-start | bytes 2097152 | tf_op jit(solution)/shard_map/all_to_all | solution.py:78
  42.5 25.5 %all-to-all-start.2 = ((f32[16,1,16384]{2,1,0:T(1,128)}), f32[16,1,16384]{2,1,0:T(1,128)}, u32[]{:S(2)}, u32[]{:S(2)}) async-start(f32[16,1,16384]{2,1,0:T(1,128)} %reshape.178), calls=%async_computation.2 | async-start | bytes 2097152 | tf_op jit(solution)/shard_map/all_to_all | solution.py:78
  68.0 26.8 %all-to-all-start.1 = ((f32[4,1,65536]{2,1,0:T(1,128)}), f32[4,1,65536]{2,1,0:T(1,128)}, u32[]{:S(2)}, u32[]{:S(2)}) async-start(f32[4,1,65536]{2,1,0:T(1,128)} %reshape.184), calls=%async_computation.1 | async-start | bytes 2097152 | tf_op jit(solution)/shard_map/all_to_all | solution.py:81
  90.6 15.0 %copy-start.17 = (s32[512]{0:T(512)S(1)}, s32[512]{0:T(512)}, u32[]{:S(2)}) copy-start(s32[512]{0:T(512)} %param.11) | copy-start | bytes 6148
  94.8 29.8 %all-to-all-start.3 = ((f32[4,1,65536]{2,1,0:T(1,128)}), f32[4,1,65536]{2,1,0:T(1,128)}, u32[]{:S(2)}, u32[]{:S(2)}) async-start(f32[4,1,65536]{2,1,0:T(1,128)} %reshape.180), calls=%async_computation.3 | async-start | bytes 2097152 | tf_op jit(solution)/shard_map/all_to_all | solution.py:81
  105.5 293.9 %all-reduce.2.cloned.1.call-start = ((), (), s32[]{:S(2)}) async-start(), calls=%async_computation.8 | async-start | bytes 524288 | tf_op jit(solution)/shard_map/psum | solution.py:95
  123.4 6.7 %copy-start.2 = (f32[16,64,256]{2,1,0:T(8,128)}, f32[16,64,256]{2,1,0:T(8,128)S(1)}, u32[]{:S(2)}) copy-start(f32[16,64,256]{2,1,0:T(8,128)S(1)} %fusion.27) | copy-start | bytes 3145732
  144.8 5.2 copy-start.4
  158.3 2.9 copy-start.16
  210.3 5.8 %copy-start.15 = (f32[8,8]{1,0:T(8,128)S(1)}, f32[8,8]{1,0:T(8,128)}, u32[]{:S(2)}) copy-start(f32[8,8]{1,0:T(8,128)} %param.13) | copy-start | bytes 772
  431.0 3.0 copy-start.3
  431.0 3.0 copy-start.5
  431.0 3.0 copy-start.14
  436.1 1.3 copy-start.8
  441.9 8.6 %copy-start.9 = (f32[2,16,64,256]{3,2,1,0:T(8,128)S(1)}, f32[2,16,64,256]{3,2,1,0:T(8,128)}, u32[]{:S(2)}) copy-start(f32[2,16,64,256]{3,2,1,0:T(8,128)} %copy-done.8) | copy-start | bytes 6291460
  446.3 29.9 %all-to-all-start.4 = ((f32[4,1,65536]{2,1,0:T(1,128)}), f32[4,1,65536]{2,1,0:T(1,128)}, u32[]{:S(2)}, u32[]{:S(2)}) async-start(f32[4,1,65536]{2,1,0:T(1,128)} %reshape.190), calls=%async_computation.4 | async-start | bytes 2097152 | tf_op jit(solution)/shard_map/all_to_all | solution.py:108
  476.2 31.3 %all-to-all-start.6 = ((f32[4,1,65536]{2,1,0:T(1,128)}), f32[4,1,65536]{2,1,0:T(1,128)}, u32[]{:S(2)}, u32[]{:S(2)}) async-start(f32[4,1,65536]{2,1,0:T(1,128)} %reshape.186), calls=%async_computation.6 | async-start | bytes 2097152 | tf_op jit(solution)/shard_map/all_to_all | solution.py:108
  507.5 21.7 %all-to-all-start.5 = ((f32[16,1,16384]{2,1,0:T(1,128)}), f32[16,1,16384]{2,1,0:T(1,128)}, u32[]{:S(2)}, u32[]{:S(2)}) async-start(f32[16,1,16384]{2,1,0:T(1,128)} %reshape.192), calls=%async_computation.5 | async-start | bytes 2097152 | tf_op jit(solution)/shard_map/all_to_all | solution.py:111
  529.2 21.7 %all-to-all-start.7 = ((f32[16,1,16384]{2,1,0:T(1,128)}), f32[16,1,16384]{2,1,0:T(1,128)}, u32[]{:S(2)}, u32[]{:S(2)}) async-start(f32[16,1,16384]{2,1,0:T(1,128)} %reshape.188), calls=%async_computation.7 | async-start | bytes 2097152 | tf_op jit(solution)/shard_map/all_to_all | solution.py:111
  557.0 4.9 copy-start.12
  557.1 4.9 copy-start.13
  557.3 4.7 copy-start.7
  557.3 4.7 copy-start.11
  562.0 2.1 copy-start.1
Sparse Core Ops, SparseCore 0:
  216.2 183.1 all-reduce.1
where the time goes:
time: 580 us; the launch traced here: 571 us
  waiting for transfers between devices  223 us (38%)
  local copies, waits for them, and re-layouts  119 us (21%)
  other arithmetic  115 us (20%)
  starting transfers between devices  51.5 us (9%)
  matrix products  48.2 us (8%)
  between operations  14.2 us (2%)
    psum x1, waiting for transfers between devices, shards(): totals = lax.psum(atom_terms, ('py', 'pz'))  183 us
    scatter-add x1, other arithmetic, shards(): atom_terms = jax.ops.segment_sum(partial_terms, atoms, num_segments=NATOM)  49.1 us
    unnamed x53, local copies, waits for them, and re-layouts  43.3 us
    all_to_all x2, waiting for transfers between devices, shards(): lax.all_to_all(values, 'py', split_axis=3, concat_axis=2, tiled=True)  29.8 us
    all_to_all x2, starting transfers between devices, shards(): lax.all_to_all(values, 'py', split_axis=2, concat_axis=3, tiled=True)  18.2 us
    scatter-add x1, other arithmetic, shards(): placed = jax.ops.segment_sum(spread, entry_block, num_segments=block_count)  16.7 us
    dot_general x4, matrix products, along_depth(): return jnp.einsum('ka,nayx->nkyx', hartley, values, precision=HIGHEST_MODE)  15.6 us
    all_to_all x2, starting transfers between devices, shards(): lax.all_to_all(values, 'pz', split_axis=1, concat_axis=2, tiled=True)  12.9 us
  transfers between devices with their start and end apart: 9, of which 5 were waited for; matrix products, arithmetic and copies ran while one was open for 21% of the time, Pallas kernels for 0%

commit v1 on v0

v1 whole, which is shorter than its diff:
```python
import functools
import math

import jax
import jax.numpy as jnp
import numpy as np
from jax import lax
from jax.experimental import pallas as pl
from jax.experimental.pallas import tpu as pltpu
from jax.sharding import PartitionSpec as P

F32 = jnp.float32
BF16 = jnp.bfloat16
I32 = jnp.int32
MESH = pl.DeviceIdType.MESH
HIGHEST = lax.Precision.HIGHEST

NPY, NPZ = 4, 16
GRID = 256
CHUNKS = 4
ZC = 16 // CHUNKS
ENT = 512
OPPOSITE = (0, 2, 1, 4, 3)


def cas_matrix():
    index = np.arange(GRID)
    angle = (index[:, None] * index[None, :] % GRID) * (2.0 * math.pi / GRID)
    return ((np.cos(angle) + np.sin(angle)) / math.sqrt(GRID)).astype(np.float32)


def halves(table):
    high = table.astype(jnp.bfloat16)
    low = (table - high.astype(np.float32)).astype(jnp.bfloat16)
    return high, low


def tables():
    cas = cas_matrix()
    wide = np.zeros((4, 2, 64, 2, GRID), np.float32)
    for band in range(2):
        wide[:, band, :, band, :] = cas.reshape(4, 64, GRID)
    wide = wide.reshape(512, 512)
    return halves(cas) + halves(wide) + halves(np.ascontiguousarray(wide.T))


def split(values):
    high = values.astype(BF16)
    return high, (values - high.astype(F32)).astype(BF16)


NN = (((1,), (0,)), ((), ()))
NT = (((1,), (1,)), ((), ()))
TN = (((0,), (0,)), ((), ()))


def mm(a, b, dims=NN):
    return lax.dot_general(a, b, dims, preferred_element_type=F32)


def mm3(a, b, dims=NN):
    (a_high, a_low), (b_high, b_low) = a, b
    return mm(a_high, b_high, dims) + (mm(a_high, b_low, dims) + mm(a_low, b_high, dims))


def iota(shape, dim):
    return lax.broadcasted_iota(I32, shape, dim)


def freq(index):
    return jnp.minimum(index, GRID - index)


def kernel(
    coef, limit, atom, block, coupling, chi, clo, pot_any, proj_any, whi_any, wlo_any, vhi_any, vlo_any,
    out,
    pot, proj, whi, wlo, vhi, vlo,
    zt, got1, yt, got2, field, xb, got3, yb, got4,
    rows_hot, cols_hot, parity, atom_hot, gathered, spread_hi, spread_lo, terms, terms_in, coupled,
    local_sem, s1, r1, s2, r2, s3, r3, s4, r4, st, rt, sc, rc,
):
    p = lax.axis_index("py")
    q = lax.axis_index("pz")
    full = jnp.logical_or(q < 6, q > 9)

    loads = [
        pltpu.make_async_copy(src, dst, local_sem.at[k])
        for k, (src, dst) in enumerate(
            [(whi_any, whi), (wlo_any, wlo), (proj_any, proj), (pot_any, pot), (vhi_any, vhi), (vlo_any, vlo)]
        )
    ]
    for load in loads:
        load.start()

    got1[:, 96:160, :] = jnp.zeros((16, 64, 128), F32)

    barrier = pltpu.get_barrier_semaphore()
    for o in range(1, NPZ):
        pl.semaphore_signal(barrier, inc=1, device_id={"pz": lax.rem(q + o, NPZ)}, device_id_type=MESH)
    for o in range(1, NPY):
        pl.semaphore_signal(barrier, inc=1, device_id={"py": lax.rem(p + o, NPY)}, device_id_type=MESH)

    c_pair = (chi[...], clo[...])

    def inside(y):
        row = limit[pl.ds(y, 1), :].astype(F32)
        diag = jnp.where(iota((64, 64), 0) == iota((64, 64), 1), jnp.broadcast_to(row, (64, 64)), 0.0)
        bound = mm(diag.astype(BF16), jnp.ones((64, GRID), BF16))
        return freq(iota((64, GRID), 1)).astype(F32) <= bound

    zt_rows = zt.reshape(4096, 128)

    def depth_step(y, carry):
        keep = inside(y)
        pair = jnp.concatenate([jnp.where(keep, coef[0, y], 0.0), jnp.where(keep, coef[1, y], 0.0)], axis=0)
        zt_rows[pl.ds(y, GRID, stride=16), :] = mm3(c_pair, split(pair), NT)
        return carry

    lax.fori_loop(0, 16, depth_step, 0)

    pl.semaphore_wait(barrier, NPZ + NPY - 2)

    def copy1(c, t, src_q, height):
        return pltpu.make_async_remote_copy(
            src_ref=zt.at[pl.ds(16 * t + ZC * c, ZC), pl.ds(0, height), :],
            dst_ref=got1.at[pl.ds(ZC * c, ZC), pl.ds(pl.multiple_of(16 * src_q, 16), height), :],
            send_sem=s1.at[c, t],
            recv_sem=r1.at[c, src_q],
            device_id={"pz": t},
            device_id_type=MESH,
        )

    def each_peer(action):
        def step(o, carry):
            action(lax.rem(q + o, NPZ))
            return carry

        lax.fori_loop(1, NPZ, step, 0)

    def ends1(c, action):
        @pl.when(full)
        def _():
            each_peer(lambda t: action(copy1(c, t, q, 16)))

        @pl.when(q == 6)
        def _():
            each_peer(lambda t: action(copy1(c, t, q, 8)))

    for c in range(CHUNKS):
        ends1(c, lambda copy: copy.start())
    got1[:, pl.ds(pl.multiple_of(16 * q, 16), 16), :] = zt[pl.ds(16 * q, 16), :, :]

    def wait1(c):
        def step(o, carry):
            t = lax.rem(q + o, NPZ)

            @pl.when(jnp.logical_or(t < 6, t > 9))
            def _():
                copy1(c, q, t, 16).wait_recv()

            @pl.when(t == 6)
            def _():
                copy1(c, q, t, 8).wait_recv()

            return carry

        lax.fori_loop(1, NPZ, step, 0)

    block_row = block[...]
    row_of = lax.shift_right_logical(block_row, 1)
    for k in range(8):
        hot = iota((128, ENT), 0) + 128 * k == jnp.broadcast_to(row_of, (128, ENT))
        rows_hot[128 * k : 128 * k + 128, :] = jnp.where(hot, 1.0, 0.0).astype(BF16)

    eye = iota((ENT, ENT), 0) == iota((ENT, ENT), 1)

    def to_column(row):
        diag = jnp.where(eye, jnp.broadcast_to(row.astype(F32), (ENT, ENT)), 0.0)
        return mm(diag.astype(BF16), jnp.ones((ENT, 128), BF16))

    row_col = 32.0 * to_column(lax.shift_right_logical(row_of, 5)) + to_column(row_of & 31)
    for k in range(8):
        hot = (iota((ENT, 128), 1) + 128 * k).astype(F32) == row_col
        cols_hot[:, 128 * k : 128 * k + 128] = jnp.where(hot, 1.0, 0.0).astype(BF16)
    parity[...] = to_column(block_row & 1)

    atoms = atom[...]
    owner = lax.shift_right_logical(atoms, 6)
    dp = (lax.shift_right_logical(owner, 4) - p) & 3
    dq = ((owner & 15) - q) & 15
    slot = jnp.where(dp == 3, 1, jnp.where(dp == 1, 2, jnp.where(dq == 15, 3, jnp.where(dq == 1, 4, 0))))
    code = slot * 64 + (atoms & 63)
    hot = iota((320, ENT), 0) == jnp.broadcast_to(code, (320, ENT))
    atom_hot[...] = jnp.where(hot, 1.0, 0.0).astype(BF16)

    def rows_pass(c, src, dst):
        def step(i, carry):
            z = ZC * c + 2 * i
            both = jnp.concatenate([src[z], src[z + 1]], axis=1)
            done = mm3(c_pair, split(both))
            dst[z] = done[:, :128]
            dst[z + 1] = done[:, 128:]
            return carry

        lax.fori_loop(0, ZC // 2, step, 0)

    def copy2(c, t, src_p):
        return pltpu.make_async_remote_copy(
            src_ref=yt.at[pl.ds(ZC * c, ZC), pl.ds(pl.multiple_of(64 * t, 64), 64), :],
            dst_ref=got2.at[src_p, pl.ds(ZC * c, ZC), :, :],
            send_sem=s2.at[c, t],
            recv_sem=r2.at[c, src_p],
            device_id={"py": t},
            device_id_type=MESH,
        )

    for c in range(CHUNKS):
        wait1(c)
        rows_pass(c, got1, yt)
        for o in (2, 1, 3):
            copy2(c, lax.rem(p + o, NPY), p).start()
        got2[p, ZC * c : ZC * c + ZC] = yt[ZC * c : ZC * c + ZC, pl.ds(pl.multiple_of(64 * p, 64), 64), :]

    loads[0].wait()
    loads[1].wait()
    height = 64 * ZC
    w_pair = (whi[...], wlo[...])
    for c in range(CHUNKS):
        for o in range(1, NPY):
            copy2(c, p, lax.rem(p + o, NPY)).wait_recv()
        lines = jnp.concatenate([got2[k, ZC * c : ZC * c + ZC].reshape(height, 128) for k in range(NPY)], axis=1)
        real = mm3(split(lines), w_pair)
        field[height * c : height * c + height, :] = real
        high, low = split(real)
        hot = cols_hot[:, height * c : height * c + height]
        part = mm(hot, high) + mm(hot, low)
        if c == 0:
            gathered[...] = part
        else:
            gathered[...] += part

    loads[2].wait()
    proj_rows = proj.reshape(ENT * 8, 128)
    odd = parity[...] > 0.5
    lane = iota((256, 128), 1)
    entry_terms = jnp.zeros((ENT, 128), F32)
    for n in range(2):
        cells = jnp.where(odd, gathered[:, 256 * n + 128 : 256 * n + 256], gathered[:, 256 * n : 256 * n + 128])
        for i in range(8):
            high, low = split(proj_rows[pl.ds(i, ENT, stride=8), :] * cells)
            column = jnp.where(lane == 8 * n + i, 1.0, 0.0).astype(BF16)
            entry_terms += mm(jnp.concatenate([high, low], axis=1), column)
    high, low = split(entry_terms)
    hot = atom_hot[...]
    terms[...] = (mm(hot, high) + mm(hot, low)).reshape(5, 64, 128)

    def neighbour(s):
        if s < 3:
            return {"py": lax.rem(p + (3 if s == 1 else 1), NPY)}
        return {"pz": lax.rem(q + (15 if s == 3 else 1), NPZ)}

    def copy_terms(s):
        return pltpu.make_async_remote_copy(
            src_ref=terms.at[s], dst_ref=terms_in.at[OPPOSITE[s]], send_sem=st.at[s], recv_sem=rt.at[OPPOSITE[s]],
            device_id=neighbour(s), device_id_type=MESH,
        )

    def copy_coupled(s):
        return pltpu.make_async_remote_copy(
            src_ref=coupled.at[0], dst_ref=coupled.at[OPPOSITE[s]], send_sem=sc.at[s], recv_sem=rc.at[OPPOSITE[s]],
            device_id=neighbour(s), device_id_type=MESH,
        )

    for s in range(1, 5):
        copy_terms(s).start()
    symmetric = 0.5 * (coupling[...] + coupling[...].T)
    place = jnp.where((iota((128, 8), 0) & 7) == iota((128, 8), 1), 1.0, 0.0)
    tiled = jnp.dot(jnp.dot(place, symmetric, precision=HIGHEST), place.T, precision=HIGHEST)
    same = lax.shift_right_logical(iota((128, 128), 0), 3) == lax.shift_right_logical(iota((128, 128), 1), 3)
    mix = jnp.where(same, tiled, 0.0)
    total = terms[0]
    for s in range(1, 5):
        copy_terms(OPPOSITE[s]).wait_recv()
        total = total + terms_in[s]
    coupled[0] = jnp.dot(total, mix, precision=HIGHEST)
    for s in range(1, 5):
        copy_coupled(s).start()
    for s in range(1, 5):
        copy_coupled(OPPOSITE[s]).wait_recv()
    high, low = split(coupled[...].reshape(320, 128))
    chosen = mm(hot, high, TN) + mm(hot, low, TN)
    for n in range(2):
        cells = jnp.zeros((ENT, 128), F32)
        for i in range(8):
            j = 8 * n + i
            weight = jnp.broadcast_to(chosen[:, j : j + 1], (ENT, 128))
            cells += proj_rows[pl.ds(i, ENT, stride=8), :] * weight
        high, low = split(cells)
        zero = jnp.zeros_like(high)
        keep = odd.astype(F32).astype(BF16) > 0.5
        spread_hi[:, 256 * n : 256 * n + 128] = jnp.where(keep, zero, high)
        spread_hi[:, 256 * n + 128 : 256 * n + 256] = jnp.where(keep, high, zero)
        spread_lo[:, 256 * n : 256 * n + 128] = jnp.where(keep, zero, low)
        spread_lo[:, 256 * n + 128 : 256 * n + 256] = jnp.where(keep, low, zero)

    def copy3(c, t, src_p):
        return pltpu.make_async_remote_copy(
            src_ref=xb.at[t, pl.ds(ZC * c, ZC), :, :],
            dst_ref=got3.at[pl.ds(ZC * c, ZC), pl.ds(pl.multiple_of(64 * src_p, 64), 64), :],
            send_sem=s3.at[c, t],
            recv_sem=r3.at[c, src_p],
            device_id={"py": t},
            device_id_type=MESH,
        )

    loads[3].wait()
    loads[4].wait()
    loads[5].wait()
    v_pair = (vhi[...], vlo[...])
    for c in range(CHUNKS):
        rows = slice(height * c, height * c + height)
        hot = rows_hot[rows, :]
        placed = mm(hot, spread_hi[...]) + mm(hot, spread_lo[...])
        local = pot[ZC * c : ZC * c + ZC].reshape(height, GRID)
        whole = jnp.concatenate([local, local], axis=1) * field[rows, :] + placed
        done = mm3(split(whole), v_pair)
        for k in range(NPY):
            xb[k, ZC * c : ZC * c + ZC] = done[:, 128 * k : 128 * k + 128].reshape(ZC, 64, 128)
        for o in (2, 1, 3):
            copy3(c, lax.rem(p + o, NPY), p).start()
        got3[ZC * c : ZC * c + ZC, pl.ds(pl.multiple_of(64 * p, 64), 64), :] = xb[p, ZC * c : ZC * c + ZC]

    def copy4(c, t, src_q, height):
        return pltpu.make_async_remote_copy(
            src_ref=yb.at[pl.ds(ZC * c, ZC), pl.ds(pl.multiple_of(16 * t, 16), height), :],
            dst_ref=got4.at[pl.ds(16 * src_q + ZC * c, ZC), pl.ds(0, height), :],
            send_sem=s4.at[c, t],
            recv_sem=r4.at[c, src_q],
            device_id={"pz": t},
            device_id_type=MESH,
        )

    def ends4(c, action):
        def one(t):
            @pl.when(jnp.logical_or(t < 6, t > 9))
            def _():
                action(copy4(c, t, q, 16))

            @pl.when(t == 6)
            def _():
                action(copy4(c, t, q, 8))

        each_peer(one)

    for c in range(CHUNKS):
        for o in range(1, NPY):
            copy3(c, p, lax.rem(p + o, NPY)).wait_recv()
        rows_pass(c, got3, yb)
        ends4(c, lambda copy: copy.start())
    got4[pl.ds(16 * q, 16), :, :] = yb[:, pl.ds(pl.multiple_of(16 * q, 16), 16), :]
    for c in range(CHUNKS):

        @pl.when(full)
        def _():
            each_peer(lambda t: copy4(c, q, t, 16).wait_recv())

        @pl.when(q == 6)
        def _():
            each_peer(lambda t: copy4(c, q, t, 8).wait_recv())

    got4_rows = got4.reshape(4096, 128)

    def final_step(y, carry):
        keep = inside(y)
        lines = got4_rows[pl.ds(y, GRID, stride=16), :]
        done = mm3(split(lines), c_pair, TN)
        fy = freq(16 * q + y)
        fx = freq(64 * p + iota((64, GRID), 0))
        fz = freq(iota((64, GRID), 1))
        kinetic = (fz * fz + fx * fx + fy * fy).astype(F32) * (0.5 * (4.0 / GRID) ** 2)
        for n in range(2):
            out[n, y] = jnp.where(keep, kinetic * coef[n, y] + done[64 * n : 64 * n + 64, :], 0.0)
        return carry

    lax.fori_loop(0, 16, final_step, 0)

    for c in range(CHUNKS):
        ends1(c, lambda copy: copy.wait_send())
        ends4(c, lambda copy: copy.wait_send())
        for o in range(1, NPY):
            t = lax.rem(p + o, NPY)
            copy2(c, t, p).wait_send()
            copy3(c, t, p).wait_send()
    for s in range(1, 5):
        copy_terms(s).wait_send()
        copy_coupled(s).wait_send()


def shards(coefficients, potential, column_limit, entry_atom, entry_block, projectors, coupling):
    vmem = pl.BlockSpec(memory_space=pltpu.VMEM)
    anywhere = pl.BlockSpec(memory_space=pl.ANY)
    big = pltpu.VMEM((16, 256, 128), F32)
    dma = pltpu.SemaphoreType.DMA
    return pl.pallas_call(
        kernel,
        name="hamiltonian",
        out_shape=jax.ShapeDtypeStruct(coefficients.shape, F32),
        in_specs=[vmem] * 7 + [anywhere] * 6,
        out_specs=vmem,
        scratch_shapes=[
            pltpu.VMEM((16, 64, GRID), F32),
            pltpu.VMEM((ENT, 8, 128), F32),
            pltpu.VMEM((512, 512), BF16),
            pltpu.VMEM((512, 512), BF16),
            pltpu.VMEM((512, 512), BF16),
            pltpu.VMEM((512, 512), BF16),
            pltpu.VMEM((256, 16, 128), F32),
            big,
            big,
            pltpu.VMEM((NPY, 16, 64, 128), F32),
            pltpu.VMEM((1024, 512), F32),
            pltpu.VMEM((NPY, 16, 64, 128), F32),
            big,
            big,
            pltpu.VMEM((256, 16, 128), F32),
            pltpu.VMEM((1024, ENT), BF16),
            pltpu.VMEM((ENT, 1024), BF16),
            pltpu.VMEM((ENT, 128), F32),
            pltpu.VMEM((320, ENT), BF16),
            pltpu.VMEM((ENT, 512), F32),
            pltpu.VMEM((ENT, 512), BF16),
            pltpu.VMEM((ENT, 512), BF16),
            pltpu.VMEM((5, 64, 128), F32),
            pltpu.VMEM((5, 64, 128), F32),
            pltpu.VMEM((5, 64, 128), F32),
            dma((6,)),
            dma((CHUNKS, NPZ)),
            dma((CHUNKS, NPZ)),
            dma((CHUNKS, NPY)),
            dma((CHUNKS, NPY)),
            dma((CHUNKS, NPY)),
            dma((CHUNKS, NPY)),
            dma((CHUNKS, NPZ)),
            dma((CHUNKS, NPZ)),
            dma((5,)),
            dma((5,)),
            dma((5,)),
            dma((5,)),
        ],
        compiler_params=pltpu.CompilerParams(
            collective_id=0, has_side_effects=True, vmem_limit_bytes=56 * 2**20
        ),
    )(
        coefficients,
        column_limit,
        entry_atom.reshape(1, ENT),
        entry_block.reshape(1, ENT),
        coupling,
        *(jnp.asarray(t) for t in tables()[:2]),
        potential,
        projectors,
        *(jnp.asarray(t) for t in tables()[2:]),
    )


def solution(mesh):
    in_specs = (
        P("band", "pz", "py", None),
        P("pz", "py", None),
        P("pz", "py"),
        P(("py", "pz"), None),
        P(("py", "pz")),
        P(("py", "pz"), None, None),
        P(),
    )
    out_specs = P("band", "pz", "py", None)
    return jax.shard_map(shards, mesh=mesh, in_specs=in_specs, out_specs=out_specs, check_vma=False)
```

time: 580 us -> 179 us (0.31); the launches traced: 571 us -> 179 us
  waiting for transfers between devices: 223 us -> 0 us
  Pallas kernels: 0 us -> 176 us
  local copies, waits for them, and re-layouts: 119 us -> 3.13 us
  other arithmetic: 115 us -> 0 us
  starting transfers between devices: 51.5 us -> 0 us
  matrix products: 48.2 us -> 0 us
  between operations: 14.2 us -> 0.01 us
    psum x1 -> x0, waiting for transfers between devices: 183 us -> none  [shards(): totals = lax.psum(atom_terms, ('py', 'pz'))]
    pallas_call x0 -> x1, Pallas kernels: none -> 176 us  [shards(): pl.pallas_call(kernel, name='hamiltonian', out_shape=jax.ShapeDtypeStruct...]
    scatter-add x2 -> x0, other arithmetic: 65.8 us -> none  [the longest x1 49.1 us: shards(): atom_terms = jax.ops.segment_sum(partial_terms, atoms, num_segments=NATOM)]
    all_to_all x8 -> x0, starting transfers between devices: 51.5 us -> none  [the longest x2 18.2 us: shards(): lax.all_to_all(values, 'py', split_axis=2, concat_axis=3, tiled=True)]
    dot_general x15 -> x0, matrix products: 48.2 us -> none  [the longest x4 15.6 us: along_depth(): return jnp.einsum('ka,nayx->nkyx', hartley, values, precision=HIGHEST_MODE)]
    unnamed x53 -> x1, local copies, waits for them, and re-layouts: 43.3 us -> 3.13 us
    all_to_all x8 -> x0, waiting for transfers between devices: 39.3 us -> none  [the longest x2 29.8 us: shards(): lax.all_to_all(values, 'py', split_axis=3, concat_axis=2, tiled=True)]
    all_to_all x8 -> x0, other arithmetic: 36.9 us -> none  [the longest x2 10.2 us: shards(): lax.all_to_all(values, 'py', split_axis=2, concat_axis=3, tiled=True)]
  transfers between devices with their start and end apart: 9 -> 0, of which waited for: 5 -> 0; matrix products, arithmetic and copies ran while one was open for 21% -> 0% of each run, Pallas kernels for 0% -> 0%
where the time goes in v1:
time: 179 us
  Pallas kernels  176 us (98%)
  local copies, waits for them, and re-layouts  3.13 us (2%)
    pallas_call x1, Pallas kernels, shards(): pl.pallas_call(kernel, name='hamiltonian', out_shape=jax.ShapeDtypeStruct...  176 us

profile of v1, /device:TPU:1, one launch (start us, length us, event | category | flops | bytes accessed | tf_op | source)
XLA Modules:
  0.0 178.9 jit_solution(13269706068002417243)
XLA Ops:
  0.0 175.8 %hamiltonian.1 = f32[2,16,64,256]{3,2,1,0:T(8,128)} custom-call(f32[2,16,64,256]{3,2,1,0:T(8,128)} %coef.1, s32[16,64]{1,0:T(8,128)} %limit.1, s32[1,512]{1,0:T(1,128)} %bitcast.2, s32[1,512]{1,0:T(1,128)} %bitcast.3, f32[8,8]{1,0:T(8,128)} %coupling.1, bf16[256,256]{1,0:T(8,128)(2,1)} %constant.12.clone.chi, bf16[256,256]{1,0:T(8,128)(2,1)} %constant.13.clone.clo, ...), custom_call_target="tpu_custom_call" | custom-call | tf_op jit(solution)/shard_map/hamiltonian/pallas_call | solution.py:404
  175.8 3.1 %copy.15 = f32[2,16,64,256]{3,2,1,0:T(8,128)} copy(f32[2,16,64,256]{3,2,1,0:T(8,128)} %hamiltonian.1) | data formatting | bytes 4194304

commit v2 on v1

v2 whole, which is shorter than its diff:
```python
import functools
import math

import jax
import jax.numpy as jnp
import numpy as np
from jax import lax
from jax.experimental import pallas as pl
from jax.experimental.pallas import tpu as pltpu
from jax.sharding import PartitionSpec as P

F32 = jnp.float32
BF16 = jnp.bfloat16
I32 = jnp.int32
MESH = pl.DeviceIdType.MESH
HIGHEST = lax.Precision.HIGHEST

NPY, NPZ = 4, 16
GRID = 256
CHUNKS = 8
ZC = 2
ROWS = 64 * ZC
ENT = 512
OPPOSITE = (0, 2, 1, 4, 3)


def cas_matrix():
    index = np.arange(GRID)
    angle = (index[:, None] * index[None, :] % GRID) * (2.0 * math.pi / GRID)
    return ((np.cos(angle) + np.sin(angle)) / math.sqrt(GRID)).astype(np.float32)


def halves(table):
    high = table.astype(jnp.bfloat16)
    low = (table - high.astype(np.float32)).astype(jnp.bfloat16)
    return high, low


def split(values):
    high = values.astype(BF16)
    return high, (values - high.astype(F32)).astype(BF16)


NN = (((1,), (0,)), ((), ()))
NT = (((1,), (1,)), ((), ()))
TN = (((0,), (0,)), ((), ()))


def mm(a, b, dims=NN):
    return lax.dot_general(a, b, dims, preferred_element_type=F32)


def mm3(a, b, dims=NN):
    (a_high, a_low), (b_high, b_low) = a, b
    return mm(a_high, b_high, dims) + (mm(a_high, b_low, dims) + mm(a_low, b_high, dims))


def iota(shape, dim):
    return lax.broadcasted_iota(I32, shape, dim)


def freq(index):
    return jnp.minimum(index, GRID - index)


def kernel(
    limit, atom, block, coupling, chi, clo, coef_any, pot_any, proj_any,
    out_any,
    coef, pot, proj, result,
    zt, got1, yt, got2, field, xb, got3, yb, got4,
    rows_hot, cols_hot, parity, atom_hot, gathered, spread_hi, spread_lo, terms, terms_in, coupled,
    local_sem, coef_sem, out_sem, send_sem, r1, r2, r3, r4, st, rt, sc, rc,
):
    p = lax.axis_index("py")
    q = lax.axis_index("pz")
    full = jnp.logical_or(q < 6, q > 9)

    coef_loads = [
        pltpu.make_async_copy(coef_any.at[:, 4 * k : 4 * k + 4], coef.at[:, 4 * k : 4 * k + 4], coef_sem.at[k])
        for k in range(4)
    ]
    loads = [
        pltpu.make_async_copy(proj_any, proj, local_sem.at[0]),
        pltpu.make_async_copy(pot_any, pot, local_sem.at[1]),
    ]
    for load in coef_loads + loads:
        load.start()

    got1[:, 96:160, :] = jnp.zeros((16, 64, 128), F32)

    barrier = pltpu.get_barrier_semaphore()
    for o in range(1, NPZ):
        pl.semaphore_signal(barrier, inc=1, device_id={"pz": lax.rem(q + o, NPZ)}, device_id_type=MESH)
    for o in range(1, NPY):
        pl.semaphore_signal(barrier, inc=1, device_id={"py": lax.rem(p + o, NPY)}, device_id_type=MESH)

    def table():
        return chi[...], clo[...]

    def apart(work):
        pl.when(q >= 0)(work)

    def inside(y):
        row = limit[pl.ds(y, 1), :].astype(F32)
        diag = jnp.where(iota((64, 64), 0) == iota((64, 64), 1), jnp.broadcast_to(row, (64, 64)), 0.0)
        bound = mm(diag.astype(BF16), jnp.ones((64, GRID), BF16))
        return freq(iota((64, GRID), 1)).astype(F32) <= bound

    zt_rows = zt.reshape(4096, 128)

    def depth_step(y, carry):
        keep = inside(y)
        pair = jnp.concatenate([jnp.where(keep, coef[0, y], 0.0), jnp.where(keep, coef[1, y], 0.0)], axis=0)
        zt_rows[pl.ds(y, GRID, stride=16), :] = mm3(table(), split(pair), NT)
        return carry

    for k in range(4):
        coef_loads[k].wait()
        lax.fori_loop(4 * k, 4 * k + 4, depth_step, 0, unroll=4)

    pl.semaphore_wait(barrier, NPZ + NPY - 2)

    def arrived(buffer, units, semaphore):
        pltpu.make_async_remote_copy(
            src_ref=buffer.at[pl.ds(0, units)], dst_ref=buffer.at[pl.ds(0, units)], send_sem=send_sem.at[0],
            recv_sem=semaphore, device_id={"pz": q}, device_id_type=MESH,
        ).wait_recv()

    def left(buffer, units, semaphore):
        pltpu.make_async_remote_copy(
            src_ref=buffer.at[pl.ds(0, units)], dst_ref=buffer.at[pl.ds(0, units)], send_sem=semaphore,
            recv_sem=r1.at[0], device_id={"pz": q}, device_id_type=MESH,
        ).wait_send()

    def each_peer(action):
        def step(o, carry):
            action(lax.rem(q + o, NPZ))
            return carry

        lax.fori_loop(1, NPZ, step, 0)

    def start1(c, t, height):
        pltpu.make_async_remote_copy(
            src_ref=zt.at[pl.ds(16 * t + ZC * c, ZC), pl.ds(0, height), :],
            dst_ref=got1.at[pl.ds(ZC * c, ZC), pl.ds(pl.multiple_of(16 * q, 16), height), :],
            send_sem=send_sem.at[0],
            recv_sem=r1.at[c],
            device_id={"pz": t},
            device_id_type=MESH,
        ).start()

    @pl.when(full)
    def _():
        for c in range(CHUNKS):
            each_peer(lambda t: start1(c, t, 16))

    @pl.when(q == 6)
    def _():
        for c in range(CHUNKS):
            each_peer(lambda t: start1(c, t, 8))

    got1[:, pl.ds(pl.multiple_of(16 * q, 16), 16), :] = zt[pl.ds(16 * q, 16), :, :]

    def by_place(when_full, when_half, when_empty):
        pl.when(full)(when_full)
        pl.when(q == 6)(when_half)
        pl.when(jnp.logical_and(q > 6, q < 10))(when_empty)

    def wait1(c):
        by_place(
            lambda: arrived(zt, 11 * ZC + ZC // 2, r1.at[c]),
            lambda: arrived(zt, 12 * ZC, r1.at[c]),
            lambda: arrived(zt, 12 * ZC + ZC // 2, r1.at[c]),
        )

    def rows_pass(c, src, dst):
        z = ZC * c
        done = mm3(table(), split(jnp.concatenate([src[z], src[z + 1]], axis=1)))
        dst[z] = done[:, :128]
        dst[z + 1] = done[:, 128:]

    def start2(c, t):
        pltpu.make_async_remote_copy(
            src_ref=yt.at[pl.ds(ZC * c, ZC), pl.ds(pl.multiple_of(64 * t, 64), 64), :],
            dst_ref=got2.at[p, pl.ds(ZC * c, ZC), :, :],
            send_sem=send_sem.at[1],
            recv_sem=r2.at[c],
            device_id={"py": t},
            device_id_type=MESH,
        ).start()

    def rows_step(c):
        wait1(c)
        rows_pass(c, got1, yt)
        for o in (2, 1, 3):
            start2(c, lax.rem(p + o, NPY))
        got2[p, ZC * c : ZC * c + ZC] = yt[ZC * c : ZC * c + ZC, pl.ds(pl.multiple_of(64 * p, 64), 64), :]

    def wait_py(c, semaphore):
        pltpu.make_async_remote_copy(
            src_ref=got2.at[pl.ds(0, 3), pl.ds(0, ZC)], dst_ref=got2.at[pl.ds(0, 3), pl.ds(0, ZC)],
            send_sem=send_sem.at[1], recv_sem=semaphore, device_id={"py": p}, device_id_type=MESH,
        ).wait_recv()

    lower = iota((ROWS, 128), 1) < 64

    def swap(values):
        return pltpu.roll(values, 64, 1)

    def width_step(c):
        wait_py(c, r2.at[c])
        part = [got2[k, ZC * c : ZC * c + ZC].reshape(ROWS, 128) for k in range(NPY)]
        turned = [swap(value) for value in part]
        first = [jnp.where(lower, part[k], turned[k + 1]) for k in (0, 2)]
        second = [jnp.where(lower, turned[k], part[k + 1]) for k in (0, 2)]
        lines = jnp.concatenate([jnp.concatenate(first, axis=1), jnp.concatenate(second, axis=1)], axis=0)
        real = mm3(split(lines), table())
        field[ROWS * c : ROWS * c + ROWS, :GRID] = real[:ROWS]
        field[ROWS * c : ROWS * c + ROWS, GRID:] = real[ROWS:]

    def gather(c0, c1):
        high, low = split(field[ROWS * c0 : ROWS * c1, :])
        hot = cols_hot[:, ROWS * c0 : ROWS * c1]
        part = mm(hot, high) + mm(hot, low)
        if c0 == 0:
            gathered[...] = part
        else:
            gathered[...] += part

    def one_hot_tables():
        block_row = block[...]
        row_of = lax.shift_right_logical(block_row, 1)
        for k in range(8):
            hot = iota((128, ENT), 0) + 128 * k == jnp.broadcast_to(row_of, (128, ENT))
            rows_hot[128 * k : 128 * k + 128, :] = jnp.where(hot, 1.0, 0.0).astype(BF16)

        eye = iota((ENT, ENT), 0) == iota((ENT, ENT), 1)

        def to_column(row):
            diag = jnp.where(eye, jnp.broadcast_to(row.astype(F32), (ENT, ENT)), 0.0)
            return mm(diag.astype(BF16), jnp.ones((ENT, 128), BF16))

        row_col = 32.0 * to_column(lax.shift_right_logical(row_of, 5)) + to_column(row_of & 31)
        for k in range(8):
            hot = (iota((ENT, 128), 1) + 128 * k).astype(F32) == row_col
            cols_hot[:, 128 * k : 128 * k + 128] = jnp.where(hot, 1.0, 0.0).astype(BF16)
        parity[...] = to_column(block_row & 1)

        atoms = atom[...]
        owner = lax.shift_right_logical(atoms, 6)
        dp = (lax.shift_right_logical(owner, 4) - p) & 3
        dq = ((owner & 15) - q) & 15
        slot = jnp.where(dp == 3, 1, jnp.where(dp == 1, 2, jnp.where(dq == 15, 3, jnp.where(dq == 1, 4, 0))))
        code = slot * 64 + (atoms & 63)
        hot = iota((320, ENT), 0) == jnp.broadcast_to(code, (320, ENT))
        atom_hot[...] = jnp.where(hot, 1.0, 0.0).astype(BF16)

    proj_rows = proj.reshape(ENT * 8, 128)
    lane = iota((ENT, 128), 1)

    def neighbour(s):
        if s < 3:
            return {"py": lax.rem(p + (3 if s == 1 else 1), NPY)}
        return {"pz": lax.rem(q + (15 if s == 3 else 1), NPZ)}

    def copy_terms(rnd, s):
        return pltpu.make_async_remote_copy(
            src_ref=terms.at[rnd, s], dst_ref=terms_in.at[rnd, OPPOSITE[s]], send_sem=st.at[rnd, s],
            recv_sem=rt.at[rnd, OPPOSITE[s]], device_id=neighbour(s), device_id_type=MESH,
        )

    def copy_coupled(rnd, s):
        return pltpu.make_async_remote_copy(
            src_ref=coupled.at[rnd, 0], dst_ref=coupled.at[rnd, OPPOSITE[s]], send_sem=sc.at[rnd, s],
            recv_sem=rc.at[rnd, OPPOSITE[s]], device_id=neighbour(s), device_id_type=MESH,
        )

    def send_terms(rnd):
        odd = parity[...] > 0.5
        entry_terms = jnp.zeros((ENT, 128), F32)
        if rnd == 0:
            whole = gathered[...]
        else:
            high, low = split(field[ROWS * 5 :, :])
            hot = cols_hot[:, ROWS * 5 :]
            whole = gathered[...] + (mm(hot, high) + mm(hot, low))
        for n in range(2):
            cells = jnp.where(odd, whole[:, 256 * n + 128 : 256 * n + 256], whole[:, 256 * n : 256 * n + 128])
            for i in range(8):
                high, low = split(proj_rows[pl.ds(i, ENT, stride=8), :] * cells)
                sums = mm(jnp.concatenate([high, low], axis=1), jnp.ones((256, 128), BF16))
                entry_terms = jnp.where(lane == 8 * n + i, sums, entry_terms)
        high, low = split(entry_terms)
        hot = atom_hot[...]
        terms[rnd] = (mm(hot, high) + mm(hot, low)).reshape(5, 64, 128)
        for s in range(1, 5):
            copy_terms(rnd, s).start()

    def send_coupled(rnd):
        symmetric = 0.5 * (coupling[...] + coupling[...].T)
        place = jnp.where((iota((128, 8), 0) & 7) == iota((128, 8), 1), 1.0, 0.0)
        tiled = jnp.dot(jnp.dot(place, symmetric, precision=HIGHEST), place.T, precision=HIGHEST)
        same = lax.shift_right_logical(iota((128, 128), 0), 3) == lax.shift_right_logical(iota((128, 128), 1), 3)
        mix = jnp.where(same, tiled, 0.0)
        total = terms[rnd, 0]
        for s in range(1, 5):
            copy_terms(rnd, OPPOSITE[s]).wait_recv()
            total = total + terms_in[rnd, s]
        coupled[rnd, 0] = jnp.dot(total, mix, precision=HIGHEST)
        for s in range(1, 5):
            copy_coupled(rnd, s).start()

    def spread_coupled(rnd):
        for s in range(1, 5):
            copy_coupled(rnd, OPPOSITE[s]).wait_recv()
        odd = parity[...]
        hot = atom_hot[...]
        high, low = split(coupled[rnd].reshape(320, 128))
        chosen = mm(hot, high, TN) + mm(hot, low, TN)
        for n in range(2):
            cells = jnp.zeros((ENT, 128), F32)
            for i in range(8):
                j = 8 * n + i
                weight = jnp.broadcast_to(chosen[:, j : j + 1], (ENT, 128))
                cells += proj_rows[pl.ds(i, ENT, stride=8), :] * weight
            for half in range(2):
                high, low = split(jnp.where(odd > 0.5, cells if half else 0.0, 0.0 if half else cells))
                lanes = slice(256 * n + 128 * half, 256 * n + 128 * half + 128)
                spread_hi[:, lanes] = high
                spread_lo[:, lanes] = low

    def start3(c, t):
        pltpu.make_async_remote_copy(
            src_ref=xb.at[t, pl.ds(ZC * c, ZC), :, :],
            dst_ref=got3.at[pl.ds(ZC * c, ZC), pl.ds(pl.multiple_of(64 * p, 64), 64), :],
            send_sem=send_sem.at[2],
            recv_sem=r3.at[c],
            device_id={"py": t},
            device_id_type=MESH,
        ).start()

    def back_step(c0, c1):
        rows = slice(ROWS * c0, ROWS * c1)
        hot = rows_hot[rows, :]
        placed = mm(hot, spread_hi[...]) + mm(hot, spread_lo[...])
        count = ROWS * (c1 - c0)
        local = pot[ZC * c0 : ZC * c1].reshape(count, GRID)
        whole = [local * field[rows, GRID * n : GRID * n + GRID] + placed[:, GRID * n : GRID * n + GRID] for n in range(2)]
        done = mm3(split(jnp.concatenate(whole, axis=0)), table())
        for c in range(c0, c1):
            top = ROWS * (c - c0)
            for h in range(2):
                first = done[top : top + ROWS, 128 * h : 128 * h + 128]
                second = done[count + top : count + top + ROWS, 128 * h : 128 * h + 128]
                xb[2 * h, ZC * c : ZC * c + ZC] = jnp.where(lower, first, swap(second)).reshape(ZC, 64, 128)
                xb[2 * h + 1, ZC * c : ZC * c + ZC] = jnp.where(lower, swap(first), second).reshape(ZC, 64, 128)
            for o in (2, 1, 3):
                start3(c, lax.rem(p + o, NPY))
            got3[ZC * c : ZC * c + ZC, pl.ds(pl.multiple_of(64 * p, 64), 64), :] = xb[p, ZC * c : ZC * c + ZC]

    def start4(c, t, height):
        pltpu.make_async_remote_copy(
            src_ref=yb.at[pl.ds(ZC * c, ZC), pl.ds(pl.multiple_of(16 * t, 16), height), :],
            dst_ref=got4.at[pl.ds(16 * q + ZC * c, ZC), pl.ds(0, height), :],
            send_sem=send_sem.at[3],
            recv_sem=r4,
            device_id={"pz": t},
            device_id_type=MESH,
        ).start()

    def final_rows(c):
        wait_py(c, r3.at[c])
        rows_pass(c, got3, yb)

        def one(t):
            @pl.when(jnp.logical_or(t < 6, t > 9))
            def _():
                start4(c, t, 16)

            @pl.when(t == 6)
            def _():
                start4(c, t, 8)

        each_peer(one)

    apart(one_hot_tables)
    for c in range(CHUNKS):
        apart(functools.partial(rows_step, c))
    for load in loads:
        load.wait()
    apart(functools.partial(width_step, 0))
    apart(functools.partial(width_step, 1))
    apart(functools.partial(gather, 0, 2))
    apart(functools.partial(width_step, 2))
    apart(functools.partial(width_step, 3))
    apart(functools.partial(gather, 2, 4))
    apart(functools.partial(width_step, 4))
    apart(functools.partial(gather, 4, 5))
    apart(functools.partial(send_terms, 0))
    apart(functools.partial(width_step, 5))
    apart(functools.partial(send_coupled, 0))
    apart(functools.partial(width_step, 6))
    apart(functools.partial(spread_coupled, 0))
    apart(functools.partial(back_step, 1, 2))
    apart(functools.partial(back_step, 2, 4))
    apart(functools.partial(width_step, 7))
    apart(functools.partial(send_terms, 1))
    apart(functools.partial(final_rows, 1))
    apart(functools.partial(send_coupled, 1))
    apart(functools.partial(final_rows, 2))
    apart(functools.partial(spread_coupled, 1))
    apart(functools.partial(back_step, 4, 6))
    apart(functools.partial(back_step, 6, 8))
    apart(functools.partial(back_step, 0, 1))
    for c in (3, 4, 5, 6, 7, 0):
        apart(functools.partial(final_rows, c))
    got4[pl.ds(16 * q, 16), :, :] = yb[:, pl.ds(pl.multiple_of(16 * q, 16), 16), :]

    pl.when(full)(lambda: left(zt, 15 * 16, send_sem.at[0]))
    pl.when(q == 6)(lambda: left(zt, 15 * 8, send_sem.at[0]))
    for k in (1, 2):
        pltpu.make_async_remote_copy(
            src_ref=got2.at[pl.ds(0, 3)], dst_ref=got2.at[pl.ds(0, 3)], send_sem=send_sem.at[k], recv_sem=r2.at[0],
            device_id={"py": p}, device_id_type=MESH,
        ).wait_send()
    for rnd in range(2):
        for s in range(1, 5):
            copy_terms(rnd, s).wait_send()
            copy_coupled(rnd, s).wait_send()

    pl.when(full)(lambda: arrived(zt, 15 * 16, r4))
    pl.when(q == 6)(lambda: arrived(zt, 15 * 8, r4))

    got4_rows = got4.reshape(4096, 128)

    def final_step(y, carry):
        keep = inside(y)
        lines = got4_rows[pl.ds(y, GRID, stride=16), :]
        done = mm3(split(lines), table(), TN)
        fy = freq(16 * q + y)
        fx = freq(64 * p + iota((64, GRID), 0))
        fz = freq(iota((64, GRID), 1))
        kinetic = (fz * fz + fx * fx + fy * fy).astype(F32) * (0.5 * (4.0 / GRID) ** 2)
        for n in range(2):
            result[n, y] = jnp.where(keep, kinetic * coef[n, y] + done[64 * n : 64 * n + 64, :], 0.0)
        return carry

    writes = []
    for k in range(4):
        lax.fori_loop(4 * k, 4 * k + 4, final_step, 0, unroll=4)
        writes.append(
            pltpu.make_async_copy(result.at[:, 4 * k : 4 * k + 4], out_any.at[:, 4 * k : 4 * k + 4], out_sem.at[k])
        )
        writes[-1].start()
    by_place(
        lambda: left(zt, 11 * 16 + 8, send_sem.at[3]),
        lambda: left(zt, 12 * 16, send_sem.at[3]),
        lambda: left(zt, 12 * 16 + 8, send_sem.at[3]),
    )
    for write in writes:
        write.wait()


def shards(coefficients, potential, column_limit, entry_atom, entry_block, projectors, coupling):
    vmem = pl.BlockSpec(memory_space=pltpu.VMEM)
    anywhere = pl.BlockSpec(memory_space=pl.ANY)
    big = pltpu.VMEM((16, 256, 128), F32)
    dma = pltpu.SemaphoreType.DMA
    return pl.pallas_call(
        kernel,
        name="hamiltonian",
        out_shape=jax.ShapeDtypeStruct(coefficients.shape, F32),
        in_specs=[vmem] * 6 + [anywhere] * 3,
        out_specs=anywhere,
        scratch_shapes=[
            pltpu.VMEM((2, 16, 64, GRID), F32),
            pltpu.VMEM((16, 64, GRID), F32),
            pltpu.VMEM((ENT, 8, 128), F32),
            pltpu.VMEM((2, 16, 64, GRID), F32),
            pltpu.VMEM((256, 16, 128), F32),
            big,
            big,
            pltpu.VMEM((NPY, 16, 64, 128), F32),
            pltpu.VMEM((1024, 512), F32),
            pltpu.VMEM((NPY, 16, 64, 128), F32),
            big,
            big,
            pltpu.VMEM((256, 16, 128), F32),
            pltpu.VMEM((1024, ENT), BF16),
            pltpu.VMEM((ENT, 1024), BF16),
            pltpu.VMEM((ENT, 128), F32),
            pltpu.VMEM((320, ENT), BF16),
            pltpu.VMEM((ENT, 512), F32),
            pltpu.VMEM((ENT, 512), BF16),
            pltpu.VMEM((ENT, 512), BF16),
            pltpu.VMEM((2, 5, 64, 128), F32),
            pltpu.VMEM((2, 5, 64, 128), F32),
            pltpu.VMEM((2, 5, 64, 128), F32),
            dma((2,)),
            dma((4,)),
            dma((4,)),
            dma((4,)),
            dma((CHUNKS,)),
            dma((CHUNKS,)),
            dma((CHUNKS,)),
            dma,
            dma((2, 5)),
            dma((2, 5)),
            dma((2, 5)),
            dma((2, 5)),
        ],
        compiler_params=pltpu.CompilerParams(
            collective_id=0, has_side_effects=True, vmem_limit_bytes=56 * 2**20
        ),
    )(
        column_limit,
        entry_atom.reshape(1, ENT),
        entry_block.reshape(1, ENT),
        coupling,
        *(jnp.asarray(table) for table in halves(cas_matrix())),
        coefficients,
        potential,
        projectors,
    )


def solution(mesh):
    in_specs = (
        P("band", "pz", "py", None),
        P("pz", "py", None),
        P("pz", "py"),
        P(("py", "pz"), None),
        P(("py", "pz")),
        P(("py", "pz"), None, None),
        P(),
    )
    out_specs = P("band", "pz", "py", None)
    return jax.shard_map(shards, mesh=mesh, in_specs=in_specs, out_specs=out_specs, check_vma=False)
```

time: 179 us -> 169 us (0.944)
  Pallas kernels: 176 us -> 166 us
    pallas_call x1, Pallas kernels: 176 us -> 166 us  [shards(): pl.pallas_call(kernel, name='hamiltonian', out_shape=jax.ShapeDtypeStruct...]
where the time goes in v2:
time: 169 us
  Pallas kernels  166 us (98%)
  local copies, waits for them, and re-layouts  3.13 us (2%)
    pallas_call x1, Pallas kernels, shards(): pl.pallas_call(kernel, name='hamiltonian', out_shape=jax.ShapeDtypeStruct...  166 us

profile of v2, /device:TPU:1, one launch (start us, length us, event | category | flops | bytes accessed | tf_op | source)
XLA Modules:
  0.0 168.9 jit_solution(1763032660540084268)
XLA Ops:
  0.0 165.8 %hamiltonian.1 = f32[2,16,64,256]{3,2,1,0:T(8,128)} custom-call(s32[16,64]{1,0:T(8,128)} %limit.1, s32[1,512]{1,0:T(1,128)} %bitcast.2, s32[1,512]{1,0:T(1,128)} %bitcast.3, f32[8,8]{1,0:T(8,128)} %coupling.1, bf16[256,256]{1,0:T(8,128)(2,1)} %constant.4.clone.chi, bf16[256,256]{1,0:T(8,128)(2,1)} %constant.5.clone.clo, f32[2,16,64,256]{3,2,1,0:T(8,128)} %coef_any.1, ...), custom_call_target="tpu_custom_call" | custom-call | tf_op jit(solution)/shard_map/hamiltonian/pallas_call | solution.py:469
  165.8 3.1 %copy.11 = f32[2,16,64,256]{3,2,1,0:T(8,128)} copy(f32[2,16,64,256]{3,2,1,0:T(8,128)} %hamiltonian.1) | data formatting | bytes 4194304

commit v3 on v2

--- a/solution.py
+++ b/solution.py
@@ -189,11 +189,13 @@
             device_id_type=MESH,
         ).start()
 
+    def send2(c):
+        for o in (1, 3, 2):
+            start2(c, lax.rem(p + o, NPY))
+
     def rows_step(c):
         wait1(c)
         rows_pass(c, got1, yt)
-        for o in (2, 1, 3):
-            start2(c, lax.rem(p + o, NPY))
         got2[p, ZC * c : ZC * c + ZC] = yt[ZC * c : ZC * c + ZC, pl.ds(pl.multiple_of(64 * p, 64), 64), :]
 
     def wait_py(c, semaphore):
@@ -339,6 +341,10 @@
             device_id_type=MESH,
         ).start()
 
+    def send3(c):
+        for o in (1, 3, 2):
+            start3(c, lax.rem(p + o, NPY))
+
     def back_step(c0, c1):
         rows = slice(ROWS * c0, ROWS * c1)
         hot = rows_hot[rows, :]
@@ -354,8 +360,6 @@
                 second = done[count + top : count + top + ROWS, 128 * h : 128 * h + 128]
                 xb[2 * h, ZC * c : ZC * c + ZC] = jnp.where(lower, first, swap(second)).reshape(ZC, 64, 128)
                 xb[2 * h + 1, ZC * c : ZC * c + ZC] = jnp.where(lower, swap(first), second).reshape(ZC, 64, 128)
-            for o in (2, 1, 3):
-                start3(c, lax.rem(p + o, NPY))
             got3[ZC * c : ZC * c + ZC, pl.ds(pl.multiple_of(64 * p, 64), 64), :] = xb[p, ZC * c : ZC * c + ZC]
 
     def start4(c, t, height):
@@ -372,6 +376,7 @@
         wait_py(c, r3.at[c])
         rows_pass(c, got3, yb)
 
+    def send4(c):
         def one(t):
             @pl.when(jnp.logical_or(t < 6, t > 9))
             def _():
@@ -386,34 +391,53 @@
     apart(one_hot_tables)
     for c in range(CHUNKS):
         apart(functools.partial(rows_step, c))
+        if c < 2:
+            send2(c)
     for load in loads:
         load.wait()
     apart(functools.partial(width_step, 0))
+    send2(2)
     apart(functools.partial(width_step, 1))
+    send2(3)
     apart(functools.partial(gather, 0, 2))
     apart(functools.partial(width_step, 2))
+    send2(4)
     apart(functools.partial(width_step, 3))
+    send2(5)
     apart(functools.partial(gather, 2, 4))
     apart(functools.partial(width_step, 4))
     apart(functools.partial(gather, 4, 5))
     apart(functools.partial(send_terms, 0))
+    send2(6)
     apart(functools.partial(width_step, 5))
     apart(functools.partial(send_coupled, 0))
+    send2(7)
     apart(functools.partial(width_step, 6))
     apart(functools.partial(spread_coupled, 0))
     apart(functools.partial(back_step, 1, 2))
-    apart(functools.partial(back_step, 2, 4))
+    send3(1)
     apart(functools.partial(width_step, 7))
     apart(functools.partial(send_terms, 1))
+    apart(functools.partial(back_step, 2, 4))
+    send3(2)
     apart(functools.partial(final_rows, 1))
     apart(functools.partial(send_coupled, 1))
+    send3(3)
+    send4(1)
     apart(functools.partial(final_rows, 2))
     apart(functools.partial(spread_coupled, 1))
     apart(functools.partial(back_step, 4, 6))
+    send3(4)
+    send3(5)
+    send4(2)
     apart(functools.partial(back_step, 6, 8))
+    send3(6)
+    send3(7)
     apart(functools.partial(back_step, 0, 1))
+    send3(0)
     for c in (3, 4, 5, 6, 7, 0):
         apart(functools.partial(final_rows, c))
+        send4(c)
     got4[pl.ds(16 * q, 16), :, :] = yb[:, pl.ds(pl.multiple_of(16 * q, 16), 16), :]
 
     pl.when(full)(lambda: left(zt, 15 * 16, send_sem.at[0]))

time: 169 us -> 159 us (0.941)
  Pallas kernels: 166 us -> 156 us
    pallas_call x1, Pallas kernels: 166 us -> 156 us  [shards(): pl.pallas_call(kernel, name='hamiltonian', out_shape=jax.ShapeDtypeStruct...]
where the time goes in v3:
time: 159 us
  Pallas kernels  156 us (98%)
  local copies, waits for them, and re-layouts  3.13 us (2%)
    pallas_call x1, Pallas kernels, shards(): pl.pallas_call(kernel, name='hamiltonian', out_shape=jax.ShapeDtypeStruct...  156 us

profile of v3, /device:TPU:1, one launch (start us, length us, event | category | flops | bytes accessed | tf_op | source)
XLA Modules:
  0.0 159.1 jit_solution(10365882266376300593)
XLA Ops:
  0.0 156.0 %hamiltonian.1 = f32[2,16,64,256]{3,2,1,0:T(8,128)} custom-call(s32[16,64]{1,0:T(8,128)} %limit.1, s32[1,512]{1,0:T(1,128)} %bitcast.2, s32[1,512]{1,0:T(1,128)} %bitcast.3, f32[8,8]{1,0:T(8,128)} %coupling.1, bf16[256,256]{1,0:T(8,128)(2,1)} %constant.4.clone.chi, bf16[256,256]{1,0:T(8,128)(2,1)} %constant.5.clone.clo, f32[2,16,64,256]{3,2,1,0:T(8,128)} %coef_any.1, ...), custom_call_target="tpu_custom_call" | custom-call | tf_op jit(solution)/shard_map/hamiltonian/pallas_call | solution.py:493
  156.0 3.1 %copy.11 = f32[2,16,64,256]{3,2,1,0:T(8,128)} copy(f32[2,16,64,256]{3,2,1,0:T(8,128)} %hamiltonian.1) | data formatting | bytes 4194304

commit v4 on v3

--- a/solution.py
+++ b/solution.py
@@ -63,13 +63,20 @@
     return jnp.minimum(index, GRID - index)
 
 
+def inside(limit, y):
+    row = limit[pl.ds(y, 1), :].astype(F32)
+    diag = jnp.where(iota((64, 64), 0) == iota((64, 64), 1), jnp.broadcast_to(row, (64, 64)), 0.0)
+    bound = mm(diag.astype(BF16), jnp.ones((64, GRID), BF16))
+    return freq(iota((64, GRID), 1)).astype(F32) <= bound
+
+
 def kernel(
     limit, atom, block, coupling, chi, clo, coef_any, pot_any, proj_any,
-    out_any,
-    coef, pot, proj, result,
-    zt, got1, yt, got2, field, xb, got3, yb, got4,
+    got4,
+    coef, pot, proj,
+    zt, got1, yt, got2, field, xb, got3, yb,
     rows_hot, cols_hot, parity, atom_hot, gathered, spread_hi, spread_lo, terms, terms_in, coupled,
-    local_sem, coef_sem, out_sem, send_sem, r1, r2, r3, r4, st, rt, sc, rc,
+    local_sem, coef_sem, send_sem, r1, r2, r3, r4, st, rt, sc, rc,
 ):
     p = lax.axis_index("py")
     q = lax.axis_index("pz")
@@ -100,16 +107,10 @@
     def apart(work):
         pl.when(q >= 0)(work)
 
-    def inside(y):
-        row = limit[pl.ds(y, 1), :].astype(F32)
-        diag = jnp.where(iota((64, 64), 0) == iota((64, 64), 1), jnp.broadcast_to(row, (64, 64)), 0.0)
-        bound = mm(diag.astype(BF16), jnp.ones((64, GRID), BF16))
-        return freq(iota((64, GRID), 1)).astype(F32) <= bound
-
     zt_rows = zt.reshape(4096, 128)
 
     def depth_step(y, carry):
-        keep = inside(y)
+        keep = inside(limit, y)
         pair = jnp.concatenate([jnp.where(keep, coef[0, y], 0.0), jnp.where(keep, coef[1, y], 0.0)], axis=0)
         zt_rows[pl.ds(y, GRID, stride=16), :] = mm3(table(), split(pair), NT)
         return carry
@@ -431,14 +432,26 @@
     send3(5)
     send4(2)
     apart(functools.partial(back_step, 6, 8))
+    apart(functools.partial(back_step, 0, 1))
+    apart(functools.partial(final_rows, 3))
     send3(6)
+    send4(3)
+    apart(functools.partial(final_rows, 4))
     send3(7)
-    apart(functools.partial(back_step, 0, 1))
+    send4(4)
+    apart(functools.partial(final_rows, 5))
     send3(0)
-    for c in (3, 4, 5, 6, 7, 0):
-        apart(functools.partial(final_rows, c))
-        send4(c)
-    got4[pl.ds(16 * q, 16), :, :] = yb[:, pl.ds(pl.multiple_of(16 * q, 16), 16), :]
+    send4(5)
+    apart(functools.partial(final_rows, 6))
+    send4(6)
+    apart(functools.partial(final_rows, 7))
+    send4(7)
+    apart(functools.partial(final_rows, 0))
+    send4(0)
+    own = pltpu.make_async_copy(
+        yb.at[:, pl.ds(pl.multiple_of(16 * q, 16), 16), :], got4.at[pl.ds(16 * q, 16), :, :], local_sem.at[2]
+    )
+    own.start()
 
     pl.when(full)(lambda: left(zt, 15 * 16, send_sem.at[0]))
     pl.when(q == 6)(lambda: left(zt, 15 * 8, send_sem.at[0]))
@@ -455,34 +468,33 @@
     pl.when(full)(lambda: arrived(zt, 15 * 16, r4))
     pl.when(q == 6)(lambda: arrived(zt, 15 * 8, r4))
 
-    got4_rows = got4.reshape(4096, 128)
-
-    def final_step(y, carry):
-        keep = inside(y)
-        lines = got4_rows[pl.ds(y, GRID, stride=16), :]
-        done = mm3(split(lines), table(), TN)
-        fy = freq(16 * q + y)
-        fx = freq(64 * p + iota((64, GRID), 0))
-        fz = freq(iota((64, GRID), 1))
-        kinetic = (fz * fz + fx * fx + fy * fy).astype(F32) * (0.5 * (4.0 / GRID) ** 2)
-        for n in range(2):
-            result[n, y] = jnp.where(keep, kinetic * coef[n, y] + done[64 * n : 64 * n + 64, :], 0.0)
-        return carry
-
-    writes = []
-    for k in range(4):
-        lax.fori_loop(4 * k, 4 * k + 4, final_step, 0, unroll=4)
-        writes.append(
-            pltpu.make_async_copy(result.at[:, 4 * k : 4 * k + 4], out_any.at[:, 4 * k : 4 * k + 4], out_sem.at[k])
-        )
-        writes[-1].start()
     by_place(
         lambda: left(zt, 11 * 16 + 8, send_sem.at[3]),
         lambda: left(zt, 12 * 16, send_sem.at[3]),
         lambda: left(zt, 12 * 16 + 8, send_sem.at[3]),
     )
-    for write in writes:
-        write.wait()
+    own.wait()
+
+
+def finish(limit, chi, clo, got4, coef, out):
+    p = lax.axis_index("py")
+    q = lax.axis_index("pz")
+    base = 8 * pl.program_id(0)
+    rows = got4.reshape(2048, 128)
+
+    def final_step(y, carry):
+        keep = inside(limit, base + y)
+        lines = rows[pl.ds(y, GRID, stride=8), :]
+        done = mm3(split(lines), (chi[...], clo[...]), TN)
+        fy = freq(16 * q + base + y)
+        fx = freq(64 * p + iota((64, GRID), 0))
+        fz = freq(iota((64, GRID), 1))
+        kinetic = (fz * fz + fx * fx + fy * fy).astype(F32) * (0.5 * (4.0 / GRID) ** 2)
+        for n in range(2):
+            out[n, y] = jnp.where(keep, kinetic * coef[n, y] + done[64 * n : 64 * n + 64, :], 0.0)
+        return carry
+
+    lax.fori_loop(0, 8, final_step, 0, unroll=8)
 
 
 def shards(coefficients, potential, column_limit, entry_atom, entry_block, projectors, coupling):
@@ -490,17 +502,17 @@
     anywhere = pl.BlockSpec(memory_space=pl.ANY)
     big = pltpu.VMEM((16, 256, 128), F32)
     dma = pltpu.SemaphoreType.DMA
-    return pl.pallas_call(
+    cas = [jnp.asarray(table) for table in halves(cas_matrix())]
+    columns = pl.pallas_call(
         kernel,
         name="hamiltonian",
-        out_shape=jax.ShapeDtypeStruct(coefficients.shape, F32),
+        out_shape=jax.ShapeDtypeStruct((256, 16, 128), F32),
         in_specs=[vmem] * 6 + [anywhere] * 3,
         out_specs=anywhere,
         scratch_shapes=[
             pltpu.VMEM((2, 16, 64, GRID), F32),
             pltpu.VMEM((16, 64, GRID), F32),
             pltpu.VMEM((ENT, 8, 128), F32),
-            pltpu.VMEM((2, 16, 64, GRID), F32),
             pltpu.VMEM((256, 16, 128), F32),
             big,
             big,
@@ -509,7 +521,6 @@
             pltpu.VMEM((NPY, 16, 64, 128), F32),
             big,
             big,
-            pltpu.VMEM((256, 16, 128), F32),
             pltpu.VMEM((1024, ENT), BF16),
             pltpu.VMEM((ENT, 1024), BF16),
             pltpu.VMEM((ENT, 128), F32),
@@ -520,8 +531,7 @@
             pltpu.VMEM((2, 5, 64, 128), F32),
             pltpu.VMEM((2, 5, 64, 128), F32),
             pltpu.VMEM((2, 5, 64, 128), F32),
-            dma((2,)),
-            dma((4,)),
+            dma((3,)),
             dma((4,)),
             dma((4,)),
             dma((CHUNKS,)),
@@ -541,11 +551,23 @@
         entry_atom.reshape(1, ENT),
         entry_block.reshape(1, ENT),
         coupling,
-        *(jnp.asarray(table) for table in halves(cas_matrix())),
+        *cas,
         coefficients,
         potential,
         projectors,
     )
+    whole = pl.BlockSpec((16, 64), lambda g: (0, 0))
+    square = pl.BlockSpec((GRID, GRID), lambda g: (0, 0))
+    bands = pl.BlockSpec((2, 8, 64, GRID), lambda g: (0, g, 0, 0))
+    return pl.pallas_call(
+        finish,
+        name="finish",
+        grid=(2,),
+        out_shape=jax.ShapeDtypeStruct(coefficients.shape, F32),
+        in_specs=[whole, square, square, pl.BlockSpec((256, 8, 128), lambda g: (0, g, 0)), bands],
+        out_specs=bands,
+        compiler_params=pltpu.CompilerParams(vmem_limit_bytes=60 * 2**20),
+    )(column_limit, *cas, columns, coefficients)
 
 
 def solution(mesh):

time: 159 us -> 158 us (level)
  local copies, waits for them, and re-layouts: 3.13 us -> 0 us
  Pallas kernels: 156 us -> 158 us
    pallas_call x0 -> x1, Pallas kernels: none -> 4.15 us  [shards(): pl.pallas_call(finish, name='finish', grid=(2,), out_shape=jax.ShapeDtype...]
    unnamed x1 -> x0, local copies, waits for them, and re-layouts: 3.13 us -> none
    pallas_call x1, Pallas kernels: 156 us -> 154 us  [shards(): pl.pallas_call(kernel, name='hamiltonian', out_shape=jax.ShapeDtypeStruct...]
where the time goes in v4:
time: 158 us
  Pallas kernels  158 us (100%)
    pallas_call x1, Pallas kernels, shards(): pl.pallas_call(kernel, name='hamiltonian', out_shape=jax.ShapeDtypeStruct...  154 us
    pallas_call x1, Pallas kernels, shards(): pl.pallas_call(finish, name='finish', grid=(2,), out_shape=jax.ShapeDtype...  4.15 us

profile of v4, /device:TPU:1, one launch (start us, length us, event | category | flops | bytes accessed | tf_op | source)
XLA Modules:
  0.0 157.7 jit_solution(4014206730329462460)
XLA Ops:
  0.0 153.5 %hamiltonian.1.got4 = f32[256,16,128]{2,1,0:T(8,128)} custom-call(s32[16,64]{1,0:T(8,128)} %limit.3, s32[1,512]{1,0:T(1,128)} %bitcast.2, s32[1,512]{1,0:T(1,128)} %bitcast.3, f32[8,8]{1,0:T(8,128)} %coupling.1, bf16[256,256]{1,0:T(8,128)(2,1)} %constant.4.clone.chi, bf16[256,256]{1,0:T(8,128)(2,1)} %constant.5.clone.clo, f32[2,16,64,256]{3,2,1,0:T(8,128)} %coef.1, ...), custom_call_target="tpu_custom_call" | custom-call | tf_op jit(solution)/shard_map/hamiltonian/pallas_call | solution.py:506
  153.5 4.2 %finish.1 = f32[2,16,64,256]{3,2,1,0:T(8,128)} custom-call(s32[16,64]{1,0:T(8,128)} %limit.3, bf16[256,256]{1,0:T(8,128)(2,1)} %constant.4.clone.chi, bf16[256,256]{1,0:T(8,128)(2,1)} %constant.5.clone.clo, f32[256,16,128]{2,1,0:T(8,128)} %hamiltonian.1.got4, f32[2,16,64,256]{3,2,1,0:T(8,128)} %coef.1), custom_call_target="tpu_custom_call" | custom-call | tf_op jit(solution)/shard_map/finish/pallas_call | solution.py:562

commit v5 on v4

--- a/solution.py
+++ b/solution.py
@@ -295,21 +295,24 @@
                 entry_terms = jnp.where(lane == 8 * n + i, sums, entry_terms)
         high, low = split(entry_terms)
         hot = atom_hot[...]
-        terms[rnd] = (mm(hot, high) + mm(hot, low)).reshape(5, 64, 128)
+        sums = mm(hot, high) + mm(hot, low)
+        for s in range(5):
+            square = jnp.concatenate([sums[64 * s : 64 * s + 64], jnp.zeros((64, 128), F32)], axis=0)
+            terms[rnd, s] = square.T[:16]
         for s in range(1, 5):
             copy_terms(rnd, s).start()
 
     def send_coupled(rnd):
         symmetric = 0.5 * (coupling[...] + coupling[...].T)
-        place = jnp.where((iota((128, 8), 0) & 7) == iota((128, 8), 1), 1.0, 0.0)
+        place = jnp.where((iota((16, 8), 0) & 7) == iota((16, 8), 1), 1.0, 0.0)
         tiled = jnp.dot(jnp.dot(place, symmetric, precision=HIGHEST), place.T, precision=HIGHEST)
-        same = lax.shift_right_logical(iota((128, 128), 0), 3) == lax.shift_right_logical(iota((128, 128), 1), 3)
+        same = lax.shift_right_logical(iota((16, 16), 0), 3) == lax.shift_right_logical(iota((16, 16), 1), 3)
         mix = jnp.where(same, tiled, 0.0)
         total = terms[rnd, 0]
         for s in range(1, 5):
             copy_terms(rnd, OPPOSITE[s]).wait_recv()
             total = total + terms_in[rnd, s]
-        coupled[rnd, 0] = jnp.dot(total, mix, precision=HIGHEST)
+        coupled[rnd, 0] = jnp.dot(mix, total, precision=HIGHEST)
         for s in range(1, 5):
             copy_coupled(rnd, s).start()
 
@@ -318,7 +321,9 @@
             copy_coupled(rnd, OPPOSITE[s]).wait_recv()
         odd = parity[...]
         hot = atom_hot[...]
-        high, low = split(coupled[rnd].reshape(320, 128))
+        filler = jnp.zeros((112, 128), F32)
+        squares = [jnp.concatenate([coupled[rnd, s], filler], axis=0).T[:64] for s in range(5)]
+        high, low = split(jnp.concatenate(squares, axis=0))
         chosen = mm(hot, high, TN) + mm(hot, low, TN)
         for n in range(2):
             cells = jnp.zeros((ENT, 128), F32)
@@ -528,9 +533,9 @@
             pltpu.VMEM((ENT, 512), F32),
             pltpu.VMEM((ENT, 512), BF16),
             pltpu.VMEM((ENT, 512), BF16),
-            pltpu.VMEM((2, 5, 64, 128), F32),
-            pltpu.VMEM((2, 5, 64, 128), F32),
-            pltpu.VMEM((2, 5, 64, 128), F32),
+            pltpu.VMEM((2, 5, 16, 128), F32),
+            pltpu.VMEM((2, 5, 16, 128), F32),
+            pltpu.VMEM((2, 5, 16, 128), F32),
             dma((3,)),
             dma((4,)),
             dma((4,)),

time: 158 us -> 154 us (0.975)
  Pallas kernels: 158 us -> 154 us
    pallas_call x1, Pallas kernels: 154 us -> 150 us  [shards(): pl.pallas_call(kernel, name='hamiltonian', out_shape=jax.ShapeDtypeStruct...]
where the time goes in v5:
time: 154 us
  Pallas kernels  154 us (100%)
    pallas_call x1, Pallas kernels, shards(): pl.pallas_call(kernel, name='hamiltonian', out_shape=jax.ShapeDtypeStruct...  150 us
    pallas_call x1, Pallas kernels, shards(): pl.pallas_call(finish, name='finish', grid=(2,), out_shape=jax.ShapeDtype...  4.16 us

profile of v5, /device:TPU:1, one launch (start us, length us, event | category | flops | bytes accessed | tf_op | source)
XLA Modules:
  0.0 154.0 jit_solution(10449254318624293111)
XLA Ops:
  0.0 149.8 %hamiltonian.1.got4 = f32[256,16,128]{2,1,0:T(8,128)} custom-call(s32[16,64]{1,0:T(8,128)} %limit.3, s32[1,512]{1,0:T(1,128)} %bitcast.2, s32[1,512]{1,0:T(1,128)} %bitcast.3, f32[8,8]{1,0:T(8,128)} %coupling.1, bf16[256,256]{1,0:T(8,128)(2,1)} %constant.4.clone.chi, bf16[256,256]{1,0:T(8,128)(2,1)} %constant.5.clone.clo, f32[2,16,64,256]{3,2,1,0:T(8,128)} %coef.1, ...), custom_call_target="tpu_custom_call" | custom-call | tf_op jit(solution)/shard_map/hamiltonian/pallas_call | solution.py:511
  149.8 4.2 %finish.1 = f32[2,16,64,256]{3,2,1,0:T(8,128)} custom-call(s32[16,64]{1,0:T(8,128)} %limit.3, bf16[256,256]{1,0:T(8,128)(2,1)} %constant.4.clone.chi, bf16[256,256]{1,0:T(8,128)(2,1)} %constant.5.clone.clo, f32[256,16,128]{2,1,0:T(8,128)} %hamiltonian.1.got4, f32[2,16,64,256]{3,2,1,0:T(8,128)} %coef.1), custom_call_target="tpu_custom_call" | custom-call | tf_op jit(solution)/shard_map/finish/pallas_call | solution.py:567
